TPU v7x, 256 devices: a whole 4x4x8 slice. The times are simulated.
256 devices in a mesh: row: 4 (over x_hi, core), rad: 2 (over x_lo), azi: 32 (over z, y).
Axes of the slice: x: 4 (x_hi: 2, x_lo: 2; x = x_hi * 2 + x_lo), y: 4, z: 8, core: 2. Of those that a mesh axis runs over, the one named last changes fastest.
Arguments:
- density: float32 [64, 32, 8192], P('row', 'rad', 'azi'), may hold values from 0.8 to 1.25
- velocity: float32 [3, 64, 32, 8192], P(None, 'row', 'rad', 'azi'), may hold values from -1.2 to 1.2
- pressure: float32 [64, 32, 8192], P('row', 'rad', 'azi'), may hold values from 0.6 to 1.4
- nu_tilde: float32 [64, 32, 8192], P('row', 'rad', 'azi'), may hold values from 0.02 to 0.2
- wall_distance: float32 [64, 32, 8192], P('row', 'rad', 'azi'), may hold values from 0.5 to 4
- interp_fwd: float32 [32, 32], P('rad')
- interp_back: float32 [32, 32], P('rad')
- offset: int32 [1], replicated, may hold values from 0 to 8191
Outputs:
- flow_next: float32 [6, 64, 32, 8192], P(None, 'row', 'rad', 'azi')
- shielding: float32 [64, 32, 8192], P('row', 'rad', 'azi')
All inputs are finite; a program needn't handle non-finite values.
Results may differ from a plain program's by a relative error of at most 0.00005.
Values sent between devices are 32-bit elements; how exact they have to be, the bound alone decides.
No kernel may reach another device: no remote copies, remote signals or barrier semaphores. Data moves between devices by JAX's collectives and lax.ppermute only.
A program may use at most 128 MiB of HBM per device.

v0:
```python
import functools

import jax
import jax.numpy as jnp
from jax import lax
from jax.experimental import pallas as pl
from jax.experimental.pallas import tpu as pltpu
from jax.sharding import PartitionSpec as P

GAMMA = 1.4
CFL = 0.8
KAPPA = 0.41
C_DES = 0.65
CB1 = 0.1355
CW1 = 3.239
NU_LAM = 0.001
GRAD_FLOOR = 0.2

AXES = ("row", "rad", "azi")
LANES = 128
CHUNK = 4
F32 = jnp.float32
VMEM = pl.BlockSpec(memory_space=pltpu.VMEM)
SMEM = pl.BlockSpec(memory_space=pltpu.SMEM)
HBM = pl.BlockSpec(memory_space=pltpu.HBM)


def params(mib=32):
    return pltpu.CompilerParams(vmem_limit_bytes=mib * 1024 * 1024)


def shaped(*dims):
    return jax.ShapeDtypeStruct(dims, F32)


def apart(*dims):
    return pltpu.HBM(dims, F32)


def far_away(array):
    return pltpu.with_memory_space_constraint(array, pltpu.HBM)


def sound_speed(rho, press):
    return jnp.sqrt(GAMMA * press / rho)


def energy_of(press, m, u):
    return press * (1.0 / (GAMMA - 1.0)) + 0.5 * (m[0] * u[0] + m[1] * u[1] + m[2] * u[2])


def state_of(prim):
    rho, u, press, nut = prim[0], prim[1:4], prim[4], prim[5]
    m = [rho * v for v in u]
    return dict(
        rho=rho, m=m, u=u, p=press, e=energy_of(press, m, u), n=rho * nut, c=sound_speed(rho, press)
    )


def cons_of(s):
    return [s["rho"], s["m"][0], s["m"][1], s["m"][2], s["e"], s["n"]]


def flux_of(s, k):
    w = s["u"][k]
    mom = [s["m"][k] * s["u"][i] for i in range(3)]
    mom[k] = mom[k] + s["p"]
    return [s["m"][k], mom[0], mom[1], mom[2], (s["e"] + s["p"]) * w, s["n"] * w]


def face_of(left, right, k):
    wave = jnp.maximum(jnp.abs(left["u"][k]) + left["c"], jnp.abs(right["u"][k]) + right["c"])
    return [
        (fl + fr) - wave * (ur - ul)
        for fl, fr, ul, ur in zip(
            flux_of(left, k), flux_of(right, k), cons_of(left), cons_of(right)
        )
    ]


NAMES = ("rho", "u0", "u1", "u2", "p", "m0", "m1", "m2", "e", "n", "c")
PASSED = ("rho", "u0", "u1", "u2", "p", "e", "n", "c")


def pack_state(s):
    return dict(
        rho=s["rho"], u0=s["u"][0], u1=s["u"][1], u2=s["u"][2], p=s["p"], e=s["e"], n=s["n"], c=s["c"]
    )


def unpack_state(d):
    u = [d["u0"], d["u1"], d["u2"]]
    return dict(rho=d["rho"], u=u, m=[d["rho"] * v for v in u], p=d["p"], e=d["e"], n=d["n"], c=d["c"])


def fetch(sources, prim, rows, sems):
    rho, vel, press, nut = sources
    return [
        pltpu.make_async_copy(rho.at[rows], prim.at[0, rows], sems.at[0]),
        pltpu.make_async_copy(vel.at[:, rows], prim.at[pl.ds(1, 3), rows], sems.at[1]),
        pltpu.make_async_copy(press.at[rows], prim.at[4, rows], sems.at[2]),
        pltpu.make_async_copy(nut.at[rows], prim.at[5, rows], sems.at[3]),
    ]


def derive_kernel(
    rho_in, vel_in, press_in, nut_in, core, up_send, layer, far_layer, col_down, top, prim, sems,
):
    _, count, radial, width = prim.shape
    even = lax.axis_index("row") % 2 == 0
    inner_rad = lax.axis_index("rad") == 0
    lane = lax.broadcasted_iota(jnp.int32, (radial, LANES), 1)
    parts = count // CHUNK

    def part_of(k):
        return fetch((rho_in, vel_in, press_in, nut_in), prim, pl.ds(k * CHUNK, CHUNK), sems.at[k])

    for k in range(parts):
        for c in part_of(k):
            c.start()
    up_send[:, :, width:] = jnp.zeros((6, radial, LANES), F32)
    col_down[...] = jnp.zeros(col_down.shape, F32)

    def step(a, best):
        speed = 3.0 * sound_speed(prim[0, a], prim[4, a])
        here = lane == a
        for v in range(6):
            plane = prim[v, a]
            if 1 <= v <= 3:
                speed = speed + jnp.abs(plane)
            high, low = plane[radial - 1 :], plane[:1]
            layer[v, pl.ds(a, 1), :] = jnp.where(inner_rad, high, low)
            far_layer[v, pl.ds(a, 1), :] = jnp.where(inner_rad, low, high)
            first, last = plane[:, :LANES], plane[:, width - LANES :]
            up_send[v, :, width:] = jnp.where(
                here, pltpu.roll(last, a + 1, 1), up_send[v, :, width:]
            )
            col_down[v] = jnp.where(here, pltpu.roll(first, a, 1), col_down[v])
        return jnp.maximum(best, speed)

    best = jnp.zeros((radial, width), F32)
    for k in range(parts):
        for c in part_of(k):
            c.wait()
        best = lax.fori_loop(k * CHUNK, (k + 1) * CHUNK, step, best)
    largest = jnp.max(best, axis=0, keepdims=True)
    largest = jnp.max(largest, axis=1, keepdims=True)
    for v in range(6):
        low, high = prim[v, 0], prim[v, count - 1]
        core[v] = jnp.where(even, high, low)
        up_send[v, :, :width] = jnp.where(even, low, high)
    top[...] = jnp.broadcast_to(largest.reshape(1, 1, 1), top.shape)


def shift_kernel(shift, came, sent, layer, out):
    radial, width = layer.shape[1], layer.shape[2]
    row = lax.axis_index("row")
    amount = shift[0] % width
    amount = jnp.where(row == 1, amount, jnp.where(row == 2, width - amount, 0))
    tiles = amount // LANES
    rest = amount % LANES
    lane = lax.broadcasted_iota(jnp.int32, (radial, LANES), 1)
    for v in range(6):
        parts = [
            pltpu.roll(ref[v, :, h * LANES : (h + 1) * LANES], rest, 1)
            for ref in (came, sent)
            for h in range(2)
        ]
        for t in range(2):
            picks = [
                jnp.where(lane < rest, parts[max(1 + t - q, 0)], parts[2 + t - q]) for q in range(3)
            ]
            out[v, :radial, t * LANES : (t + 1) * LANES] = jnp.where(
                tiles == 0, picks[0], jnp.where(tiles == 1, picks[1], picks[2])
            )
        out[v, radial:, :] = layer[v]


def weight_kernel(fwd, back, own, other, out):
    radial = out.shape[1]
    low = lax.axis_index("rad") == 0
    table = jnp.where(lax.axis_index("row") == 1, fwd[...], back[...])
    for v in range(6):
        mine, theirs = own[v, :radial], other[v, :radial]
        plane = jnp.concatenate([jnp.where(low, mine, theirs), jnp.where(low, theirs, mine)], 0)
        out[v] = jnp.dot(
            table, plane, precision=lax.Precision.HIGHEST, preferred_element_type=F32
        )


def closure(rho, nut, dist, grad2):
    strain = jnp.maximum(jnp.sqrt(0.25 * grad2), GRAD_FLOOR)
    ratio = (nut + NU_LAM) / (KAPPA * KAPPA * dist * dist * strain)
    eight = 8.0 * ratio
    shielding = 1.0 - jnp.tanh(eight * eight * eight)
    length = dist - shielding * jnp.maximum(0.0, dist - C_DES)
    quot = nut / length
    return shielding, rho * (CB1 * strain * nut - CW1 * (quot * quot))


def state_at(prim, der, a):
    return dict(
        rho=prim[0, a],
        u=[prim[1 + i, a] for i in range(3)],
        p=prim[4, a],
        m=[der[i, a] for i in range(3)],
        e=der[3, a],
        n=der[4, a],
        c=der[5, a],
    )


def face_kernel(
    rho_in, vel_in, press_in, nut_in, wall_in, core, layer, own_layer, wall_layer, came, col_next,
    col_own, top, flow_out, shield_out, edge_out,
    prim, der, wall, flow, shield,
    low_face, lay_hi, lay_lo, lay_u, azi_hi, azi_lo, azi_u, sems, out_sems,
):
    _, count, radial, width = prim.shape
    row, rad = lax.axis_index("row"), lax.axis_index("rad")
    even = row % 2 == 0
    at_low = rad == 0
    parts = count // CHUNK

    def part_of(k):
        rows = pl.ds(k * CHUNK, CHUNK)
        part = fetch((rho_in, vel_in, press_in, nut_in), prim, rows, sems.at[k])
        return part + [pltpu.make_async_copy(wall_in.at[rows], wall.at[rows], sems.at[k, 4])]

    def results_of(k):
        rows = pl.ds(k * CHUNK, CHUNK)
        return [
            pltpu.make_async_copy(flow.at[:, rows], flow_out.at[:, rows], out_sems.at[k, 0]),
            pltpu.make_async_copy(shield.at[rows], shield_out.at[rows], out_sems.at[k, 1]),
        ]

    for k in range(parts):
        for c in part_of(k):
            c.start()
    step_size = CFL / jnp.max(top[...])
    half = 0.5 * step_size
    sub = lax.broadcasted_iota(jnp.int32, (8, width), 0)
    lane = lax.broadcasted_iota(jnp.int32, (radial, LANES), 1)

    def derive(a):
        q = [prim[v, a] for v in range(6)]
        s = state_of(q)
        for i in range(3):
            der[i, a] = s["m"][i]
        der[3, a] = s["e"]
        der[4, a] = s["n"]
        der[5, a] = s["c"]

    def up_r(v, halo):
        lo, hi = pltpu.roll(v[:8], 7, 0), pltpu.roll(v[8:], 7, 0)
        edge = sub == 7
        return jnp.concatenate([jnp.where(edge, hi, lo), jnp.where(edge, halo, hi)], 0)

    def down_r(v, halo):
        lo, hi = pltpu.roll(v[:8], 1, 0), pltpu.roll(v[8:], 1, 0)
        edge = sub == 0
        return jnp.concatenate([jnp.where(edge, halo, lo), jnp.where(edge, lo, hi)], 0)

    def up_t(v, halo):
        lo, hi = pltpu.roll(v[:, :LANES], LANES - 1, 1), pltpu.roll(v[:, LANES:], LANES - 1, 1)
        edge = lane == LANES - 1
        return jnp.concatenate([jnp.where(edge, hi, lo), jnp.where(edge, halo, hi)], 1)

    def down_t(v, halo):
        lo, hi = pltpu.roll(v[:, :LANES], 1, 1), pltpu.roll(v[:, LANES:], 1, 1)
        edge = lane == 0
        return jnp.concatenate([jnp.where(edge, halo, lo), jnp.where(edge, lo, hi)], 1)

    def mirrored(q):
        return [q[0], q[1], -q[2], q[3], q[4], q[5]]

    got = [layer[v, radial:] for v in range(6)]
    bottom = [jnp.where(at_low, wall_layer[v], own_layer[v]) for v in range(6)]
    ceiling = [jnp.where(at_low, own_layer[v], wall_layer[v]) for v in range(6)]
    high = [jnp.where(at_low, g, w) for g, w in zip(got, mirrored(ceiling))]
    low = [jnp.where(at_low, w, g) for g, w in zip(got, mirrored(bottom))]
    high_state = pack_state(state_of(high))
    for i, name in enumerate(PASSED):
        lay_hi[i] = high_state[name]
    for i, f in enumerate(face_of(state_of(low), state_of(bottom), 1)):
        lay_lo[i] = f
    for i in range(3):
        lay_u[i] = low[1 + i]

    def column(ref, v):
        q = ref[v, :, ref.shape[2] - LANES :]
        return jnp.where(lane < count, q, 1.0)

    nxt_state = pack_state(state_of([column(col_next, v) for v in range(6)]))
    for i, name in enumerate(PASSED):
        azi_hi[i] = nxt_state[name]
    prev = [column(came, v) for v in range(6)]
    for i, f in enumerate(face_of(state_of(prev), state_of([column(col_own, v) for v in range(6)]), 2)):
        azi_lo[i] = f
    for i in range(3):
        azi_u[i] = prev[1 + i]

    end = [core[v] for v in range(6)]
    end_state = state_of(end)
    no_low = jnp.where(even, 0.0, 1.0)
    no_high = jnp.where(even, 1.0, 0.0)
    for c in part_of(0):
        c.wait()
    derive(0)
    for i, f in enumerate(face_of(end_state, state_at(prim, der, 0), 0)):
        low_face[i] = f * no_low

    def step(a, _):
        here = state_at(prim, der, a)
        last = a == count - 1
        first = a == 0
        later = jnp.minimum(a + 1, count - 1)
        earlier = jnp.maximum(a - 1, 0)
        total = [None] * 6
        derive(later)
        above = state_at(prim, der, later)
        right = dict(
            (k, [jnp.where(last, g, h) for g, h in zip(end_state[k], above[k])])
            if isinstance(above[k], list)
            else (k, jnp.where(last, end_state[k], above[k]))
            for k in above
        )
        keep = jnp.where(last, no_high, 1.0)
        for i, f in enumerate(face_of(here, right, 0)):
            f = f * keep
            total[i] = f - low_face[i]
            low_face[i] = f
        grad2 = None
        for i in range(3):
            down = jnp.where(first, end[1 + i], prim[1 + i, earlier])
            d = right["u"][i] - down
            grad2 = d * d if grad2 is None else grad2 + d * d
        outermost = jnp.where(even, first, last)
        grad2 = grad2 * jnp.where(outermost, 0.0, 1.0)
        packed = pack_state(here)
        row_of = pl.ds(a, 1)
        shifted = {n: up_r(packed[n], lay_hi[i, row_of, :]) for i, n in enumerate(PASSED)}
        face = face_of(here, unpack_state(shifted), 1)
        for i, f in enumerate(face):
            total[i] = total[i] + (f - down_r(f, lay_lo[i, row_of, :]))
        for i in range(3):
            d = shifted["u%d" % i] - down_r(here["u"][i], lay_u[i, row_of, :])
            grad2 = grad2 + d * d
        to_end = (LANES - 1) - a
        to_start = (LANES - a) % LANES
        shifted = {n: up_t(packed[n], pltpu.roll(azi_hi[i], to_end, 1)) for i, n in enumerate(PASSED)}
        face = face_of(here, unpack_state(shifted), 2)
        for i, f in enumerate(face):
            total[i] = total[i] + (f - down_t(f, pltpu.roll(azi_lo[i], to_start, 1)))
        for i in range(3):
            d = shifted["u%d" % i] - down_t(here["u"][i], pltpu.roll(azi_u[i], to_start, 1))
            grad2 = grad2 + d * d
        shielding, source = closure(here["rho"], prim[5, a], wall[a], grad2)
        cons = cons_of(here)
        for i in range(5):
            flow[i, a] = cons[i] - half * total[i]
        flow[5, a] = cons[5] - half * total[5] + step_size * source
        shield[a] = shielding

        @pl.when(outermost)
        def _():
            for i in range(6):
                edge_out[i] = cons[i] - half * total[i]
            edge_out[6] = grad2
            edge_out[7] = wall[a]
            inside = jnp.where(even, 1, count - 2)
            for i in range(3):
                edge_out[8 + i] = prim[1 + i, inside]
            edge_out[11] = jnp.zeros((radial, width), F32) + step_size

        return 0

    def part_step(k, _):
        @pl.when(k + 1 < parts)
        def _():
            for c in part_of(k + 1):
                c.wait()

        lax.fori_loop(k * CHUNK, (k + 1) * CHUNK, step, 0)
        for c in results_of(k):
            c.start()
        return 0

    lax.fori_loop(0, parts, part_step, 0)
    for k in range(parts):
        for c in results_of(k):
            c.wait()


def edge_kernel(
    flow_in, shield_in, edge, sent, ghost, flow_out, shield_out, edge_flow, edge_shield, sems
):
    del flow_in, shield_in
    _, radial, width = ghost.shape
    count = shield_out.shape[0]
    row = lax.axis_index("row")
    even = row % 2 == 0
    coupled = (row == 1) | (row == 2)
    step_size = edge[11]
    end = jnp.where(even, 0, count - 1)
    mine = [sent[v, :, :width] for v in range(6)]
    beyond = [jnp.where(coupled, ghost[v], mine[v]) for v in range(6)]
    here, out_state = state_of(mine), state_of(beyond)
    grad2 = edge[6]
    for i in range(3):
        d = edge[8 + i] - beyond[1 + i]
        grad2 = grad2 + d * d

    def pick(p, q):
        return dict(
            (k, [jnp.where(even, x, y) for x, y in zip(p[k], q[k])])
            if isinstance(p[k], list)
            else (k, jnp.where(even, p[k], q[k]))
            for k in p
        )

    shielding, source = closure(here["rho"], mine[5], edge[7], grad2)
    edge_shield[...] = shielding
    sign = jnp.where(even, -0.5, 0.5)
    for i, f in enumerate(face_of(pick(out_state, here), pick(here, out_state), 0)):
        value = edge[i] - step_size * (sign * f)
        edge_flow[i] = value + step_size * source if i == 5 else value
    copies = [
        pltpu.make_async_copy(edge_flow, flow_out.at[:, end], sems.at[0]),
        pltpu.make_async_copy(edge_shield, shield_out.at[end], sems.at[1]),
    ]
    for c in copies:
        c.start()
    for c in copies:
        c.wait()


def body(density, velocity, pressure, nu_tilde, wall_distance, interp_fwd, interp_back, offset):
    rows, rads, cycle = (lax.axis_size(n) for n in AXES)
    count, radial, width = density.shape

    def device(row, rad, azi):
        return (row * rads + rad) * cycle + azi % cycle

    def everyone(target):
        return [
            (device(r, d, a), target(r, d, a))
            for r in range(rows)
            for d in range(rads)
            for a in range(cycle)
        ]

    plane = shaped(6, radial, width)
    wide = shaped(6, radial, width + LANES)
    column = shaped(6, radial, LANES)
    devices = rows * rads * cycle
    whole = (6, count, radial, width)
    parts = count // CHUNK
    fields = [far_away(x) for x in (density, velocity, pressure, nu_tilde)]
    dma = pltpu.SemaphoreType.DMA
    core, up_send, layer, far_layer, col_down, top = pl.pallas_call(
        derive_kernel,
        out_shape=(
            plane, wide, shaped(6, count, width), shaped(6, count, width), column,
            shaped(devices, 1, LANES),
        ),
        in_specs=[HBM] * 4,
        out_specs=(VMEM,) * 6,
        scratch_shapes=[pltpu.VMEM(whole, F32), dma((parts, 4))],
        compiler_params=params(),
        name="derive",
    )(*fields)

    up = everyone(lambda r, d, a: device(r, d, a + 1))
    down = everyone(lambda r, d, a: device(r, d, a - 1))
    pair = everyone(lambda r, d, a: device(r ^ 1, d, a))
    across = everyone(lambda r, d, a: device(r, rads - 1 - d, a))
    tops = lax.all_to_all(top, AXES, 0, 0)
    came = lax.ppermute(up_send, AXES, up)
    col_next = lax.ppermute(col_down, AXES, down)
    core_got = lax.ppermute(core, AXES, pair)

    moved = pl.pallas_call(
        shift_kernel,
        out_shape=shaped(6, radial + count, width),
        in_specs=[SMEM, VMEM, VMEM, VMEM],
        out_specs=VMEM,
        compiler_params=params(),
        name="shift",
    )(offset, came, up_send, layer)
    swapped = lax.ppermute(moved, AXES, across)
    weighted = pl.pallas_call(
        weight_kernel,
        out_shape=plane,
        in_specs=[VMEM] * 4,
        out_specs=VMEM,
        compiler_params=params(),
        name="weigh",
    )(interp_fwd, interp_back, moved, swapped)

    faces = pl.pallas_call(
        face_kernel,
        out_shape=(apart(*whole), apart(count, radial, width), shaped(12, radial, width)),
        in_specs=[HBM] * 5 + [VMEM] * 8,
        out_specs=(HBM, HBM, VMEM),
        scratch_shapes=[
            pltpu.VMEM(whole, F32),
            pltpu.VMEM(whole, F32),
            pltpu.VMEM((count, radial, width), F32),
            pltpu.VMEM(whole, F32),
            pltpu.VMEM((count, radial, width), F32),
            pltpu.VMEM((6, radial, width), F32),
            pltpu.VMEM((8, count, width), F32),
            pltpu.VMEM((6, count, width), F32),
            pltpu.VMEM((3, count, width), F32),
            pltpu.VMEM((8, radial, LANES), F32),
            pltpu.VMEM((6, radial, LANES), F32),
            pltpu.VMEM((3, radial, LANES), F32),
            dma((parts, 5)),
            dma((parts, 2)),
        ],
        compiler_params=params(),
        cost_estimate=pl.CostEstimate(
            flops=25_000_000, bytes_accessed=6_000_000, transcendentals=300_000
        ),
        name="faces",
    )

    def far(blocks):
        route = []
        for d in range(rads):
            for a in range(cycle):
                route.append((device(1, d, a), device(2, d, a + blocks)))
                route.append((device(2, d, a), device(1, d, a + cycle - 1 - blocks)))

        def branch(block, arrays, *rest):
            return lax.ppermute(block, AXES, route), faces(*map(far_away, arrays), *rest)

        return branch

    ghost, (flow, shield, edge) = lax.switch(
        offset[0] // width,
        [far(b) for b in range(cycle)],
        weighted, (density, velocity, pressure, nu_tilde, wall_distance),
        core_got, swapped, layer, far_layer, came, col_next, col_down, tops,
    )

    return pl.pallas_call(
        edge_kernel,
        out_shape=(shaped(*whole), shaped(count, radial, width)),
        in_specs=[HBM] * 2 + [VMEM] * 3,
        out_specs=(HBM, HBM),
        input_output_aliases={0: 0, 1: 1},
        scratch_shapes=[
            pltpu.VMEM((6, radial, width), F32),
            pltpu.VMEM((radial, width), F32),
            dma((2,)),
        ],
        compiler_params=params(),
        name="edge",
    )(far_away(flow), far_away(shield), edge, up_send, ghost)


def solution(mesh):
    placed = (
        P("row", "rad", "azi"),
        P(None, "row", "rad", "azi"),
        P("row", "rad", "azi"),
        P("row", "rad", "azi"),
        P("row", "rad", "azi"),
        P("rad", None),
        P("rad", None),
        P(),
    )
    return jax.shard_map(
        body,
        mesh=mesh,
        in_specs=placed,
        out_specs=(P(None, "row", "rad", "azi"), P("row", "rad", "azi")),
        check_vma=False,
    )
```

profile of v0, /device:TPU:1, one launch (start us, length us, event | category | flops | bytes accessed | tf_op | source)
XLA Modules:
  0.0 51.0 jit_solution(9093913108882392383)
XLA Ops:
  0.6 0.0 copy-start.1
  0.6 0.0 copy-start
  0.6 3.4 %derive.1 = (f32[6,16,256]{2,1,0:T(8,128)S(1)}, f32[6,16,384]{2,1,0:T(8,128)S(1)}, f32[6,16,256]{2,1,0:T(8,128)S(1)}, f32[6,16,256]{2,1,0:T(8,128)S(1)}, f32[6,1...) custom-call(f32[16,16,256]{2,1,0:T(8,128)} %rho_in.1, f32[3,16,16,256]{3,2,1,0:T(8,128)} %vel_in.1, f32[16,16,256]{2,1,0:T(8,128)} %press_in.1, ...), custom_call_target="tpu_custom_call" | custom-call | tf_op jit(solution)/shard_map/derive/pallas_call | solution.py:461
  4.1 2.2 %collective-permute-start.32 = (f32[6,16,384]{2,1,0:T(8,128)S(1)}, f32[6,16,384]{2,1,0:T(8,128)S(1)}, u32[]{:S(2)}, u32[]{:S(2)}) collective-permute-start(f32[6,16,384]{2,1,0:T(8,128)S(1)} %get-tuple-element.1452.sent), channel_id=1, source_target_pairs={{0,1},{1,2},{2,3},{3,4},{4,5},{5,6},{6,7},{7,8},{8,9},{9,10},{10,1... | collective-permute-start | bytes 442376 | tf_op jit(solution)/shard_map/ppermute | solution.py:479
  6.3 14.8 %all-to-all-start = ((f32[256,1,128]{2,1,0:T(1,128)}), f32[256,1,128]{2,1,0:T(1,128)S(1)}, u32[]{:S(2)}, u32[]{:S(2)}) async-start(f32[256,1,128]{2,1,0:T(1,128)} %get-tuple-element.1457), calls=%async_computation | async-start | bytes 262144 | tf_op jit(solution)/shard_map/all_to_all | solution.py:478
  21.8 0.0 collective-permute-done.32.came
  21.8 0.1 shift.2.own
  21.9 1.5 %collective-permute-start.33 = (f32[6,32,256]{2,1,0:T(8,128)S(1)}, f32[6,32,256]{2,1,0:T(8,128)S(1)}, u32[]{:S(2)}, u32[]{:S(2)}) collective-permute-start(f32[6,32,256]{2,1,0:T(8,128)S(1)} %shift.2.own), channel_id=1, source_target_pairs={{0,32},{1,33},{2,34},{3,35},{4,36},{5,37},{6,38},{7,39},{8,40},{9,... | collective-permute-start | bytes 589832 | tf_op jit(solution)/shard_map/ppermute | solution.py:491
  23.4 0.9 %collective-permute-start.34 = (f32[6,16,256]{2,1,0:T(8,128)S(1)}, f32[6,16,256]{2,1,0:T(8,128)S(1)}, u32[]{:S(2)}, u32[]{:S(2)}) collective-permute-start(f32[6,16,256]{2,1,0:T(8,128)S(1)} %get-tuple-element.1454), channel_id=1, source_target_pairs={{0,64},{1,65},{2,66},{3,67},{4,68},{5,69},{6,70},{7,71},{8,72},{9,... | collective-permute-start | bytes 294920 | tf_op jit(solution)/shard_map/ppermute | solution.py:481
  24.3 6.2 %collective-permute-start.35 = (f32[6,16,128]{2,1,0:T(8,128)S(1)}, f32[6,16,128]{2,1,0:T(8,128)S(1)}, u32[]{:S(2)}, u32[]{:S(2)}) collective-permute-start(f32[6,16,128]{2,1,0:T(8,128)S(1)} %get-tuple-element.1456), channel_id=1, source_target_pairs={{0,31},{1,0},{2,1},{3,2},{4,3},{5,4},{6,5},{7,6},{8,7},{9,8},{10,9... | collective-permute-start | bytes 147464 | tf_op jit(solution)/shard_map/ppermute | solution.py:480
  30.5 0.0 collective-permute-done.33.other
  30.5 0.0 copy-done.1
  30.5 0.0 copy-done
  30.5 0.2 weigh.1
  30.8 0.9 %collective-permute-done.35 = f32[6,16,128]{2,1,0:T(8,128)S(1)} collective-permute-done((f32[6,16,128]{2,1,0:T(8,128)S(1)}, f32[6,16,128]{2,1,0:T(8,128)S(1)}, u32[]{:S(2)}, u32[]{:S(2)}) %collective-permute-start.35) | collective-permute-done | bytes 49184 | tf_op jit(solution)/shard_map/ppermute | solution.py:480
  31.7 0.0 collective-permute-done.34
  31.7 2.5 %all-to-all-done = f32[256,1,128]{2,1,0:T(1,128)S(1)} async-done(((f32[256,1,128]{2,1,0:T(1,128)}), f32[256,1,128]{2,1,0:T(1,128)S(1)}, u32[]{:S(2)}, u32[]{:S(2)}) %all-to-all-start) | async-done | bytes 131104 | tf_op jit(solution)/shard_map/all_to_all | solution.py:478
  34.1 15.0 %conditional.1 = (f32[6,16,256]{2,1,0:T(8,128)}, f32[6,16,16,256]{3,2,1,0:T(8,128)}, f32[16,16,256]{2,1,0:T(8,128)}, f32[12,16,256]{2,1,0:T(8,128)S(1)}) conditional(s32[]{:T(128)} %clamp.3, (f32[6,16,256]{2,1,0:T(8,128)S(1)}, f32[16,16,256]{2,1,0:T(8,128)}, f32[3,16,16,256]{3,2,1,0:T(8,128)}, ...), branch_computations={%region_0.1_spmd, %region_1.2_spmd, %region_2.3_spmd, %region_3.4_... | conditional | flops 25000000 | bytes 6393288 | solution.py:541
  34.1 8.6 %collective-permute-start.19 = (f32[6,16,256]{2,1,0:T(8,128)S(1)}, f32[6,16,256]{2,1,0:T(8,128)}, u32[]{:S(2)}, u32[]{:S(2)}) collective-permute-start(f32[6,16,256]{2,1,0:T(8,128)S(1)} %get-tuple-element.1219), channel_id=1, source_target_pairs={{64,147},{128,76},{65,148},{129,77},{66,149},{130,78},{67,150},{13... | collective-permute-start | bytes 294920 | tf_op jit(solution)/shard_map/cond/branch_19_fun/ppermute | solution.py:537
  42.8 6.4 %faces.51 = (f32[6,16,16,256]{3,2,1,0:T(8,128)}, f32[16,16,256]{2,1,0:T(8,128)}, f32[12,16,256]{2,1,0:T(8,128)S(1)}) custom-call(f32[16,16,256]{2,1,0:T(8,128)} %get-tuple-element.1220.rho_in, f32[3,16,16,256]{3,2,1,0:T(8,128)} %get-tuple-element.1221.vel_in, f32[16,16,256]{2,1,0:T(8,128)} %get-tuple-element.1222.press_in, ...), custom_call_target="tpu_custom_call" | custom-call | flops 25000000 | bytes 6000000 | tf_op jit(solution)/shard_map/cond/branch_19_fun/faces/pallas_call | solution.py:537
  49.2 0.0 collective-permute-done.19
  49.2 1.7 %edge.1 = (f32[6,16,16,256]{3,2,1,0:T(8,128)}, f32[16,16,256]{2,1,0:T(8,128)}) custom-call(f32[6,16,16,256]{3,2,1,0:T(8,128)} %get-tuple-element.1458.flow_in, f32[16,16,256]{2,1,0:T(8,128)} %get-tuple-element.1459.shield_in, f32[12,16,256]{2,1,0:T(8,128)S(1)} %get-tuple-element.1460.edge, ...), custom_call_target="tpu_custom_call", output_to_operand_aliasing={{0}: (0, {}), {1}: (1, {})} | custom-call | tf_op jit(solution)/shard_map/edge/pallas_call | solution.py:548
Async XLA Ops:
  0.6 29.9 %copy-start.1 = (f32[16,32]{1,0:T(8,128)S(1)}, f32[16,32]{1,0:T(8,128)}, u32[]{:S(2)}) copy-start(f32[16,32]{1,0:T(8,128)} %back.1) | copy-start | bytes 6148
  0.6 29.9 %copy-start = (f32[16,32]{1,0:T(8,128)S(1)}, f32[16,32]{1,0:T(8,128)}, u32[]{:S(2)}) copy-start(f32[16,32]{1,0:T(8,128)} %fwd.1) | copy-start | bytes 6148
  4.1 17.7 %collective-permute-start.32 = (f32[6,16,384]{2,1,0:T(8,128)S(1)}, f32[6,16,384]{2,1,0:T(8,128)S(1)}, u32[]{:S(2)}, u32[]{:S(2)}) collective-permute-start(f32[6,16,384]{2,1,0:T(8,128)S(1)} %get-tuple-element.1452.sent), channel_id=1, source_target_pairs={{0,1},{1,2},{2,3},{3,4},{4,5},{5,6},{6,7},{7,8},{8,9},{9,10},{10,1... | collective-permute-start | bytes 442376 | tf_op jit(solution)/shard_map/ppermute | solution.py:479
  6.3 27.8 %all-to-all-start = ((f32[256,1,128]{2,1,0:T(1,128)}), f32[256,1,128]{2,1,0:T(1,128)S(1)}, u32[]{:S(2)}, u32[]{:S(2)}) async-start(f32[256,1,128]{2,1,0:T(1,128)} %get-tuple-element.1457), calls=%async_computation | async-start | bytes 262144 | tf_op jit(solution)/shard_map/all_to_all | solution.py:478
  21.9 8.6 %collective-permute-start.33 = (f32[6,32,256]{2,1,0:T(8,128)S(1)}, f32[6,32,256]{2,1,0:T(8,128)S(1)}, u32[]{:S(2)}, u32[]{:S(2)}) collective-permute-start(f32[6,32,256]{2,1,0:T(8,128)S(1)} %shift.2.own), channel_id=1, source_target_pairs={{0,32},{1,33},{2,34},{3,35},{4,36},{5,37},{6,38},{7,39},{8,40},{9,... | collective-permute-start | bytes 589832 | tf_op jit(solution)/shard_map/ppermute | solution.py:491
  23.4 8.3 %collective-permute-start.34 = (f32[6,16,256]{2,1,0:T(8,128)S(1)}, f32[6,16,256]{2,1,0:T(8,128)S(1)}, u32[]{:S(2)}, u32[]{:S(2)}) collective-permute-start(f32[6,16,256]{2,1,0:T(8,128)S(1)} %get-tuple-element.1454), channel_id=1, source_target_pairs={{0,64},{1,65},{2,66},{3,67},{4,68},{5,69},{6,70},{7,71},{8,72},{9,... | collective-permute-start | bytes 294920 | tf_op jit(solution)/shard_map/ppermute | solution.py:481
  24.3 7.4 %collective-permute-start.35 = (f32[6,16,128]{2,1,0:T(8,128)S(1)}, f32[6,16,128]{2,1,0:T(8,128)S(1)}, u32[]{:S(2)}, u32[]{:S(2)}) collective-permute-start(f32[6,16,128]{2,1,0:T(8,128)S(1)} %get-tuple-element.1456), channel_id=1, source_target_pairs={{0,31},{1,0},{2,1},{3,2},{4,3},{5,4},{6,5},{7,6},{8,7},{9,8},{10,9... | collective-permute-start | bytes 147464 | tf_op jit(solution)/shard_map/ppermute | solution.py:480
  34.1 15.0 %collective-permute-start.19 = (f32[6,16,256]{2,1,0:T(8,128)S(1)}, f32[6,16,256]{2,1,0:T(8,128)}, u32[]{:S(2)}, u32[]{:S(2)}) collective-permute-start(f32[6,16,256]{2,1,0:T(8,128)S(1)} %get-tuple-element.1219), channel_id=1, source_target_pairs={{64,147},{128,76},{65,148},{129,77},{66,149},{130,78},{67,150},{13... | collective-permute-start | bytes 294920 | tf_op jit(solution)/shard_map/cond/branch_19_fun/ppermute | solution.py:537
where the time goes:
time: 50.7 us; the launch traced here: 51 us
  starting transfers between devices  34.2 us (67%)
  Pallas kernels  11.9 us (23%)
  waiting for transfers between devices  3.39 us (7%)
  between operations  1.52 us (3%)
    all_to_all x1, starting transfers between devices, body(): tops = lax.all_to_all(top, AXES, 0, 0)  14.8 us
    ppermute x1, starting transfers between devices, branch(): lax.ppermute(block, AXES, route)  8.61 us
    pallas_call x1, Pallas kernels, branch(): faces(*map(far_away, arrays), *rest)  6.39 us
    ppermute x1, starting transfers between devices, body(): col_next = lax.ppermute(col_down, AXES, down)  6.24 us
    pallas_call x1, Pallas kernels, body(): pl.pallas_call(derive_kernel, out_shape=(plane, wide, shaped(6, count, wi...  3.44 us
    all_to_all x1, waiting for transfers between devices, body(): tops = lax.all_to_all(top, AXES, 0, 0)  2.46 us
    ppermute x1, starting transfers between devices, body(): came = lax.ppermute(up_send, AXES, up)  2.2 us
    pallas_call x1, Pallas kernels, body(): pl.pallas_call(edge_kernel, out_shape=(shaped(*whole), shaped(count, radi...  1.68 us
  transfers between devices with their start and end apart: 6, of which 2 were waited for; matrix products, arithmetic and copies ran while one was open for 0% of the time, Pallas kernels for 13%

commit v1 on v0

--- a/solution.py
+++ b/solution.py
@@ -42,7 +42,8 @@
 
 
 def sound_speed(rho, press):
-    return jnp.sqrt(GAMMA * press / rho)
+    scaled = GAMMA * press
+    return scaled * lax.rsqrt(scaled * rho)
 
 
 def energy_of(press, m, u):
@@ -104,7 +105,7 @@
 
 
 def derive_kernel(
-    rho_in, vel_in, press_in, nut_in, core, up_send, layer, far_layer, col_down, top, prim, sems,
+    rho_in, vel_in, press_in, nut_in, core, up_send, layer, far_layer, cols, top, prim, sems,
 ):
     _, count, radial, width = prim.shape
     even = lax.axis_index("row") % 2 == 0
@@ -118,12 +119,11 @@
     for k in range(parts):
         for c in part_of(k):
             c.start()
-    up_send[:, :, width:] = jnp.zeros((6, radial, LANES), F32)
-    col_down[...] = jnp.zeros(col_down.shape, F32)
+    cols[...] = jnp.zeros(cols.shape, F32)
 
     def step(a, best):
         speed = 3.0 * sound_speed(prim[0, a], prim[4, a])
-        here = lane == a
+        here = lane // 2 == a
         for v in range(6):
             plane = prim[v, a]
             if 1 <= v <= 3:
@@ -132,10 +132,8 @@
             layer[v, pl.ds(a, 1), :] = jnp.where(inner_rad, high, low)
             far_layer[v, pl.ds(a, 1), :] = jnp.where(inner_rad, low, high)
             first, last = plane[:, :LANES], plane[:, width - LANES :]
-            up_send[v, :, width:] = jnp.where(
-                here, pltpu.roll(last, a + 1, 1), up_send[v, :, width:]
-            )
-            col_down[v] = jnp.where(here, pltpu.roll(first, a, 1), col_down[v])
+            both = pltpu.roll(jnp.where(lane == 0, first, last), 2 * a + 1, 1)
+            cols[v] = jnp.where(here, both, cols[v])
         return jnp.maximum(best, speed)
 
     best = jnp.zeros((radial, width), F32)
@@ -149,6 +147,7 @@
         low, high = prim[v, 0], prim[v, count - 1]
         core[v] = jnp.where(even, high, low)
         up_send[v, :, :width] = jnp.where(even, low, high)
+        up_send[v, :, width:] = cols[v]
     top[...] = jnp.broadcast_to(largest.reshape(1, 1, 1), top.shape)
 
 
@@ -189,9 +188,10 @@
 
 
 def closure(rho, nut, dist, grad2):
-    strain = jnp.maximum(jnp.sqrt(0.25 * grad2), GRAD_FLOOR)
-    ratio = (nut + NU_LAM) / (KAPPA * KAPPA * dist * dist * strain)
-    eight = 8.0 * ratio
+    square = jnp.maximum(0.25 * grad2, GRAD_FLOOR * GRAD_FLOOR)
+    inverse = lax.rsqrt(square)
+    strain = square * inverse
+    eight = (8.0 / (KAPPA * KAPPA)) * (nut + NU_LAM) * inverse / (dist * dist)
     shielding = 1.0 - jnp.tanh(eight * eight * eight)
     length = dist - shielding * jnp.maximum(0.0, dist - C_DES)
     quot = nut / length
@@ -211,9 +211,9 @@
 
 
 def face_kernel(
-    rho_in, vel_in, press_in, nut_in, wall_in, core, layer, own_layer, wall_layer, came, col_next,
+    prim, wall_in, core, layer, own_layer, wall_layer, came, col_next,
     col_own, top, flow_out, shield_out, edge_out,
-    prim, der, wall, flow, shield,
+    der, wall, flow, shield,
     low_face, lay_hi, lay_lo, lay_u, azi_hi, azi_lo, azi_u, sems, out_sems,
 ):
     _, count, radial, width = prim.shape
@@ -224,8 +224,7 @@
 
     def part_of(k):
         rows = pl.ds(k * CHUNK, CHUNK)
-        part = fetch((rho_in, vel_in, press_in, nut_in), prim, rows, sems.at[k])
-        return part + [pltpu.make_async_copy(wall_in.at[rows], wall.at[rows], sems.at[k, 4])]
+        return [pltpu.make_async_copy(wall_in.at[rows], wall.at[rows], sems.at[k])]
 
     def results_of(k):
         rows = pl.ds(k * CHUNK, CHUNK)
@@ -289,13 +288,13 @@
 
     def column(ref, v):
         q = ref[v, :, ref.shape[2] - LANES :]
-        return jnp.where(lane < count, q, 1.0)
+        return jnp.where(lane < 2 * count, q, 1.0)
 
     nxt_state = pack_state(state_of([column(col_next, v) for v in range(6)]))
     for i, name in enumerate(PASSED):
         azi_hi[i] = nxt_state[name]
     prev = [column(came, v) for v in range(6)]
-    for i, f in enumerate(face_of(state_of(prev), state_of([column(col_own, v) for v in range(6)]), 2)):
+    for i, f in enumerate(face_of(state_of(prev), state_of([pltpu.roll(column(col_own, v), LANES - 1, 1) for v in range(6)]), 2)):
         azi_lo[i] = f
     for i in range(3):
         azi_u[i] = prev[1 + i]
@@ -346,8 +345,8 @@
         for i in range(3):
             d = shifted["u%d" % i] - down_r(here["u"][i], lay_u[i, row_of, :])
             grad2 = grad2 + d * d
-        to_end = (LANES - 1) - a
-        to_start = (LANES - a) % LANES
+        to_end = (LANES - 2) - 2 * a
+        to_start = (LANES - 2 * a) % LANES
         shifted = {n: up_t(packed[n], pltpu.roll(azi_hi[i], to_end, 1)) for i, n in enumerate(PASSED)}
         face = face_of(here, unpack_state(shifted), 2)
         for i, f in enumerate(face):
@@ -401,8 +400,8 @@
     row = lax.axis_index("row")
     even = row % 2 == 0
     coupled = (row == 1) | (row == 2)
+    end = jnp.where(even, 0, count - 1)
     step_size = edge[11]
-    end = jnp.where(even, 0, count - 1)
     mine = [sent[v, :, :width] for v in range(6)]
     beyond = [jnp.where(coupled, ghost[v], mine[v]) for v in range(6)]
     here, out_state = state_of(mine), state_of(beyond)
@@ -435,6 +434,73 @@
         c.wait()
 
 
+def derive_call(fields, devices):
+    count, radial, width = fields[0].shape
+    plane, layer = shaped(6, radial, width), shaped(6, count, width)
+    return pl.pallas_call(
+        derive_kernel,
+        out_shape=(
+            plane, shaped(6, radial, width + LANES), layer, layer, shaped(6, radial, LANES),
+            shaped(devices, 1, LANES), pltpu.VMEM((6, count, radial, width), F32),
+        ),
+        in_specs=[HBM] * 4,
+        out_specs=(VMEM,) * 7,
+        scratch_shapes=[pltpu.SemaphoreType.DMA((count // CHUNK, 4))],
+        compiler_params=params(),
+        name="derive",
+    )(*fields)
+
+
+def faces_call(*arrays):
+    whole = arrays[0].shape
+    _, count, radial, width = whole
+    parts = count // CHUNK
+    return pl.pallas_call(
+        face_kernel,
+        out_shape=(apart(*whole), apart(count, radial, width), shaped(12, radial, width)),
+        in_specs=[VMEM, HBM] + [VMEM] * 8,
+        out_specs=(HBM, HBM, VMEM),
+        scratch_shapes=[
+            pltpu.VMEM(whole, F32),
+            pltpu.VMEM((count, radial, width), F32),
+            pltpu.VMEM(whole, F32),
+            pltpu.VMEM((count, radial, width), F32),
+            pltpu.VMEM((6, radial, width), F32),
+            pltpu.VMEM((8, count, width), F32),
+            pltpu.VMEM((6, count, width), F32),
+            pltpu.VMEM((3, count, width), F32),
+            pltpu.VMEM((8, radial, LANES), F32),
+            pltpu.VMEM((6, radial, LANES), F32),
+            pltpu.VMEM((3, radial, LANES), F32),
+            pltpu.SemaphoreType.DMA((parts,)),
+            pltpu.SemaphoreType.DMA((parts, 2)),
+        ],
+        compiler_params=params(),
+        cost_estimate=pl.CostEstimate(
+            flops=25_000_000, bytes_accessed=6_000_000, transcendentals=300_000
+        ),
+        name="faces",
+    )(*arrays)
+
+
+def edge_call(flow, shield, edge, sent, ghost):
+    _, radial, width = ghost.shape
+    return pl.pallas_call(
+        edge_kernel,
+        out_shape=(shaped(*flow.shape), shaped(*shield.shape)),
+        in_specs=[HBM] * 2 + [VMEM] * 3,
+        out_specs=(HBM, HBM),
+        input_output_aliases={0: 0, 1: 1},
+        scratch_shapes=[
+            pltpu.VMEM((6, radial, width), F32),
+            pltpu.VMEM((radial, width), F32),
+            pltpu.SemaphoreType.DMA((2,)),
+        ],
+        compiler_params=params(),
+        name="edge",
+    )(flow, shield, edge, sent, ghost)
+
+
 def body(density, velocity, pressure, nu_tilde, wall_distance, interp_fwd, interp_back, offset):
     rows, rads, cycle = (lax.axis_size(n) for n in AXES)
     count, radial, width = density.shape
@@ -451,25 +517,9 @@
         ]
 
     plane = shaped(6, radial, width)
-    wide = shaped(6, radial, width + LANES)
-    column = shaped(6, radial, LANES)
     devices = rows * rads * cycle
-    whole = (6, count, radial, width)
-    parts = count // CHUNK
     fields = [far_away(x) for x in (density, velocity, pressure, nu_tilde)]
-    dma = pltpu.SemaphoreType.DMA
-    core, up_send, layer, far_layer, col_down, top = pl.pallas_call(
-        derive_kernel,
-        out_shape=(
-            plane, wide, shaped(6, count, width), shaped(6, count, width), column,
-            shaped(devices, 1, LANES),
-        ),
-        in_specs=[HBM] * 4,
-        out_specs=(VMEM,) * 6,
-        scratch_shapes=[pltpu.VMEM(whole, F32), dma((parts, 4))],
-        compiler_params=params(),
-        name="derive",
-    )(*fields)
+    core, up_send, layer, far_layer, cols, top, prim = derive_call(fields, devices)
 
     up = everyone(lambda r, d, a: device(r, d, a + 1))
     down = everyone(lambda r, d, a: device(r, d, a - 1))
@@ -477,7 +527,7 @@
     across = everyone(lambda r, d, a: device(r, rads - 1 - d, a))
     tops = lax.all_to_all(top, AXES, 0, 0)
     came = lax.ppermute(up_send, AXES, up)
-    col_next = lax.ppermute(col_down, AXES, down)
+    col_next = lax.ppermute(cols, AXES, down)
     core_got = lax.ppermute(core, AXES, pair)
 
     moved = pl.pallas_call(
@@ -498,34 +548,6 @@
         name="weigh",
     )(interp_fwd, interp_back, moved, swapped)
 
-    faces = pl.pallas_call(
-        face_kernel,
-        out_shape=(apart(*whole), apart(count, radial, width), shaped(12, radial, width)),
-        in_specs=[HBM] * 5 + [VMEM] * 8,
-        out_specs=(HBM, HBM, VMEM),
-        scratch_shapes=[
-            pltpu.VMEM(whole, F32),
-            pltpu.VMEM(whole, F32),
-            pltpu.VMEM((count, radial, width), F32),
-            pltpu.VMEM(whole, F32),
-            pltpu.VMEM((count, radial, width), F32),
-            pltpu.VMEM((6, radial, width), F32),
-            pltpu.VMEM((8, count, width), F32),
-            pltpu.VMEM((6, count, width), F32),
-            pltpu.VMEM((3, count, width), F32),
-            pltpu.VMEM((8, radial, LANES), F32),
-            pltpu.VMEM((6, radial, LANES), F32),
-            pltpu.VMEM((3, radial, LANES), F32),
-            dma((parts, 5)),
-            dma((parts, 2)),
-        ],
-        compiler_params=params(),
-        cost_estimate=pl.CostEstimate(
-            flops=25_000_000, bytes_accessed=6_000_000, transcendentals=300_000
-        ),
-        name="faces",
-    )
-
     def far(blocks):
         route = []
         for d in range(rads):
@@ -533,32 +555,20 @@
                 route.append((device(1, d, a), device(2, d, a + blocks)))
                 route.append((device(2, d, a), device(1, d, a + cycle - 1 - blocks)))
 
-        def branch(block, arrays, *rest):
-            return lax.ppermute(block, AXES, route), faces(*map(far_away, arrays), *rest)
+        def branch(block, sent, near, dist, *rest):
+            near = pltpu.with_memory_space_constraint(near, pltpu.VMEM)
+            ghost = lax.ppermute(block, AXES, route)
+            flow, shield, edge = faces_call(near, far_away(dist), *rest)
+            return edge_call(far_away(flow), far_away(shield), edge, sent, ghost)
 
         return branch
 
-    ghost, (flow, shield, edge) = lax.switch(
+    return lax.switch(
         offset[0] // width,
         [far(b) for b in range(cycle)],
-        weighted, (density, velocity, pressure, nu_tilde, wall_distance),
-        core_got, swapped, layer, far_layer, came, col_next, col_down, tops,
+        weighted, up_send, prim, wall_distance,
+        core_got, swapped, layer, far_layer, came, col_next, cols, tops,
     )
-
-    return pl.pallas_call(
-        edge_kernel,
-        out_shape=(shaped(*whole), shaped(count, radial, width)),
-        in_specs=[HBM] * 2 + [VMEM] * 3,
-        out_specs=(HBM, HBM),
-        input_output_aliases={0: 0, 1: 1},
-        scratch_shapes=[
-            pltpu.VMEM((6, radial, width), F32),
-            pltpu.VMEM((radial, width), F32),
-            dma((2,)),
-        ],
-        compiler_params=params(),
-        name="edge",
-    )(far_away(flow), far_away(shield), edge, up_send, ghost)
 
 
 def solution(mesh):

time: 50.7 us -> 49.1 us (0.968)
  Pallas kernels: 11.9 us -> 10.3 us
    pallas_call x3, Pallas kernels: 11.5 us -> 9.87 us  [the longest x1 5.77 us: faces_call(): pl.pallas_call(face_kernel, out_shape=(apart(*whole), apart(count, radial...]
  transfers between devices with their start and end apart: 6 -> 6, of which waited for: 2 -> 2; matrix products, arithmetic and copies ran while one was open for 0% -> 0% of each run, Pallas kernels for 13% -> 12%
where the time goes in v1:
time: 49.1 us; the launch traced here: 49.4 us
  starting transfers between devices  34.2 us (70%)
  Pallas kernels  10.3 us (21%)
  waiting for transfers between devices  3.38 us (7%)
  between operations  1.52 us (3%)
    all_to_all x1, starting transfers between devices, body(): tops = lax.all_to_all(top, AXES, 0, 0)  14.8 us
    ppermute x1, starting transfers between devices, branch(): ghost = lax.ppermute(block, AXES, route)  8.62 us
    ppermute x1, starting transfers between devices, body(): col_next = lax.ppermute(cols, AXES, down)  6.24 us
    pallas_call x1, Pallas kernels, faces_call(): pl.pallas_call(face_kernel, out_shape=(apart(*whole), apart(count, radial...  5.77 us
    pallas_call x1, Pallas kernels, derive_call(): pl.pallas_call(derive_kernel, out_shape=(plane, shaped(6, radial, width +...  3.33 us
    all_to_all x1, waiting for transfers between devices, body(): tops = lax.all_to_all(top, AXES, 0, 0)  2.46 us
    ppermute x1, starting transfers between devices, body(): came = lax.ppermute(up_send, AXES, up)  2.2 us
    ppermute x1, starting transfers between devices, body(): swapped = lax.ppermute(moved, AXES, across)  1.47 us
  transfers between devices with their start and end apart: 6, of which 2 were waited for; matrix products, arithmetic and copies ran while one was open for 0% of the time, Pallas kernels for 12%

profile of v1, /device:TPU:1, one launch (start us, length us, event | category | flops | bytes accessed | tf_op | source)
XLA Modules:
  0.0 49.4 jit_solution(4813581229243541811)
XLA Ops:
  0.6 0.0 copy-start.1
  0.6 0.0 copy-start
  0.7 3.3 %derive.1 = (f32[6,16,256]{2,1,0:T(8,128)S(1)}, f32[6,16,384]{2,1,0:T(8,128)S(1)}, f32[6,16,256]{2,1,0:T(8,128)S(1)}, f32[6,16,256]{2,1,0:T(8,128)S(1)}, f32[6,1...) custom-call(f32[16,16,256]{2,1,0:T(8,128)} %rho_in.1, f32[3,16,16,256]{3,2,1,0:T(8,128)} %vel_in.1, ...), custom_call_target="tpu_custom_call" | custom-call | tf_op jit(solution)/shard_map/derive/pallas_call | solution.py:440
  4.0 2.2 %collective-permute-start.33 = (f32[6,16,384]{2,1,0:T(8,128)S(1)}, f32[6,16,384]{2,1,0:T(8,128)S(1)}, u32[]{:S(2)}, u32[]{:S(2)}) collective-permute-start(f32[6,16,384]{2,1,0:T(8,128)S(1)} %get-tuple-element.1259.sent), channel_id=1, source_target_pairs={{0,1},{1,2},{2,3},{3,4},{4,5},{5,6},{6,7},{7,8},{8,9},{9,10},{10,1... | collective-permute-start | bytes 442376 | tf_op jit(solution)/shard_map/ppermute | solution.py:529
  6.2 14.8 %all-to-all-start = ((f32[256,1,128]{2,1,0:T(1,128)}), f32[256,1,128]{2,1,0:T(1,128)S(1)}, u32[]{:S(2)}, u32[]{:S(2)}) async-start(f32[256,1,128]{2,1,0:T(1,128)} %get-tuple-element.1263), calls=%async_computation | async-start | bytes 262144 | tf_op jit(solution)/shard_map/all_to_all | solution.py:528
  21.7 0.0 collective-permute-done.33.came
  21.7 0.1 shift.2.own
  21.8 1.5 %collective-permute-start.34 = (f32[6,32,256]{2,1,0:T(8,128)S(1)}, f32[6,32,256]{2,1,0:T(8,128)S(1)}, u32[]{:S(2)}, u32[]{:S(2)}) collective-permute-start(f32[6,32,256]{2,1,0:T(8,128)S(1)} %shift.2.own), channel_id=1, source_target_pairs={{0,32},{1,33},{2,34},{3,35},{4,36},{5,37},{6,38},{7,39},{8,40},{9,... | collective-permute-start | bytes 589832 | tf_op jit(solution)/shard_map/ppermute | solution.py:541
  23.3 0.9 %collective-permute-start.32 = (f32[6,16,256]{2,1,0:T(8,128)S(1)}, f32[6,16,256]{2,1,0:T(8,128)S(1)}, u32[]{:S(2)}, u32[]{:S(2)}) collective-permute-start(f32[6,16,256]{2,1,0:T(8,128)S(1)} %get-tuple-element.1258), channel_id=1, source_target_pairs={{0,64},{1,65},{2,66},{3,67},{4,68},{5,69},{6,70},{7,71},{8,72},{9,... | collective-permute-start | bytes 294920 | tf_op jit(solution)/shard_map/ppermute | solution.py:531
  24.1 6.2 %collective-permute-start.35 = (f32[6,16,128]{2,1,0:T(8,128)S(1)}, f32[6,16,128]{2,1,0:T(8,128)S(1)}, u32[]{:S(2)}, u32[]{:S(2)}) collective-permute-start(f32[6,16,128]{2,1,0:T(8,128)S(1)} %get-tuple-element.1262), channel_id=1, source_target_pairs={{0,31},{1,0},{2,1},{3,2},{4,3},{5,4},{6,5},{7,6},{8,7},{9,8},{10,9... | collective-permute-start | bytes 147464 | tf_op jit(solution)/shard_map/ppermute | solution.py:530
  30.4 0.0 collective-permute-done.34.other
  30.4 0.0 copy-done.1
  30.4 0.0 copy-done
  30.4 0.2 weigh.1
  30.6 0.9 %collective-permute-done.35 = f32[6,16,128]{2,1,0:T(8,128)S(1)} collective-permute-done((f32[6,16,128]{2,1,0:T(8,128)S(1)}, f32[6,16,128]{2,1,0:T(8,128)S(1)}, u32[]{:S(2)}, u32[]{:S(2)}) %collective-permute-start.35) | collective-permute-done | bytes 49184 | tf_op jit(solution)/shard_map/ppermute | solution.py:530
  31.6 0.0 collective-permute-done.32
  31.6 2.5 %all-to-all-done = f32[256,1,128]{2,1,0:T(1,128)S(1)} async-done(((f32[256,1,128]{2,1,0:T(1,128)}), f32[256,1,128]{2,1,0:T(1,128)S(1)}, u32[]{:S(2)}, u32[]{:S(2)}) %all-to-all-start) | async-done | bytes 131104 | tf_op jit(solution)/shard_map/all_to_all | solution.py:528
  34.0 15.2 %conditional.1 = ((f32[6,16,16,256]{3,2,1,0:T(8,128)}, f32[16,16,256]{2,1,0:T(8,128)})) conditional(s32[]{:T(128)} %clamp.3, (f32[6,16,16,256]{3,2,1,0:T(8,128)S(1)}, f32[16,16,256]{2,1,0:T(8,128)}, f32[6,16,256]{2,1,0:T(8,128)S(1)}, f32[6,32,256]{2,1,0:T(8,128)S(1)}, f32[6,16,256]{2,1,0:T(8,128)S(1)}, ...), branch_computations={%region_0.1_spmd, %region_1.2_spmd, %region_2.3_spmd, %region_3.4_... | conditional | flops 25000000 | bytes 6393264 | solution.py:566
  34.0 8.6 %collective-permute-start.19 = (f32[6,16,256]{2,1,0:T(8,128)S(1)}, f32[6,16,256]{2,1,0:T(8,128)S(1)}, u32[]{:S(2)}, u32[]{:S(2)}) collective-permute-start(f32[6,16,256]{2,1,0:T(8,128)S(1)} %get-tuple-element.1067), channel_id=1, source_target_pairs={{64,147},{128,76},{65,148},{129,77},{66,149},{130,78},{67,150},{13... | collective-permute-start | bytes 294920 | tf_op jit(solution)/shard_map/cond/branch_19_fun/ppermute | solution.py:560
  42.7 5.8 %faces.51 = (f32[6,16,16,256]{3,2,1,0:T(8,128)}, f32[16,16,256]{2,1,0:T(8,128)}, f32[12,16,256]{2,1,0:T(8,128)S(1)}) custom-call(f32[6,16,16,256]{3,2,1,0:T(8,128)S(1)} %get-tuple-element.1053.prim, f32[16,16,256]{2,1,0:T(8,128)} %get-tuple-element.1054.wall_in, f32[6,16,256]{2,1,0:T(8,128)S(1)} %get-tuple-element.1055.core, ...), custom_call_target="tpu_custom_call" | custom-call | flops 25000000 | bytes 6000000 | tf_op jit(solution)/shard_map/cond/branch_19_fun/faces/pallas_call | solution.py:458
  48.4 0.0 collective-permute-done.19.ghost
  48.4 0.8 %edge.51 = (f32[6,16,16,256]{3,2,1,0:T(8,128)}, f32[16,16,256]{2,1,0:T(8,128)}) custom-call(f32[6,16,16,256]{3,2,1,0:T(8,128)} %get-tuple-element.1063.flow_in, f32[16,16,256]{2,1,0:T(8,128)} %get-tuple-element.1064.shield_in, f32[12,16,256]{2,1,0:T(8,128)S(1)} %get-tuple-element.1065.edge, ...), custom_call_target="tpu_custom_call", output_to_operand_aliasing={{0}: (0, {}), {1}: (1, {})} | custom-call | tf_op jit(solution)/shard_map/cond/branch_19_fun/edge/pallas_call | solution.py:488
Async XLA Ops:
  0.6 29.8 %copy-start.1 = (f32[16,32]{1,0:T(8,128)S(1)}, f32[16,32]{1,0:T(8,128)}, u32[]{:S(2)}) copy-start(f32[16,32]{1,0:T(8,128)} %back.1) | copy-start | bytes 6148
  0.6 29.8 %copy-start = (f32[16,32]{1,0:T(8,128)S(1)}, f32[16,32]{1,0:T(8,128)}, u32[]{:S(2)}) copy-start(f32[16,32]{1,0:T(8,128)} %fwd.1) | copy-start | bytes 6148
  4.0 17.7 %collective-permute-start.33 = (f32[6,16,384]{2,1,0:T(8,128)S(1)}, f32[6,16,384]{2,1,0:T(8,128)S(1)}, u32[]{:S(2)}, u32[]{:S(2)}) collective-permute-start(f32[6,16,384]{2,1,0:T(8,128)S(1)} %get-tuple-element.1259.sent), channel_id=1, source_target_pairs={{0,1},{1,2},{2,3},{3,4},{4,5},{5,6},{6,7},{7,8},{8,9},{9,10},{10,1... | collective-permute-start | bytes 442376 | tf_op jit(solution)/shard_map/ppermute | solution.py:529
  6.2 27.8 %all-to-all-start = ((f32[256,1,128]{2,1,0:T(1,128)}), f32[256,1,128]{2,1,0:T(1,128)S(1)}, u32[]{:S(2)}, u32[]{:S(2)}) async-start(f32[256,1,128]{2,1,0:T(1,128)} %get-tuple-element.1263), calls=%async_computation | async-start | bytes 262144 | tf_op jit(solution)/shard_map/all_to_all | solution.py:528
  21.8 8.6 %collective-permute-start.34 = (f32[6,32,256]{2,1,0:T(8,128)S(1)}, f32[6,32,256]{2,1,0:T(8,128)S(1)}, u32[]{:S(2)}, u32[]{:S(2)}) collective-permute-start(f32[6,32,256]{2,1,0:T(8,128)S(1)} %shift.2.own), channel_id=1, source_target_pairs={{0,32},{1,33},{2,34},{3,35},{4,36},{5,37},{6,38},{7,39},{8,40},{9,... | collective-permute-start | bytes 589832 | tf_op jit(solution)/shard_map/ppermute | solution.py:541
  23.3 8.3 %collective-permute-start.32 = (f32[6,16,256]{2,1,0:T(8,128)S(1)}, f32[6,16,256]{2,1,0:T(8,128)S(1)}, u32[]{:S(2)}, u32[]{:S(2)}) collective-permute-start(f32[6,16,256]{2,1,0:T(8,128)S(1)} %get-tuple-element.1258), channel_id=1, source_target_pairs={{0,64},{1,65},{2,66},{3,67},{4,68},{5,69},{6,70},{7,71},{8,72},{9,... | collective-permute-start | bytes 294920 | tf_op jit(solution)/shard_map/ppermute | solution.py:531
  24.1 7.4 %collective-permute-start.35 = (f32[6,16,128]{2,1,0:T(8,128)S(1)}, f32[6,16,128]{2,1,0:T(8,128)S(1)}, u32[]{:S(2)}, u32[]{:S(2)}) collective-permute-start(f32[6,16,128]{2,1,0:T(8,128)S(1)} %get-tuple-element.1262), channel_id=1, source_target_pairs={{0,31},{1,0},{2,1},{3,2},{4,3},{5,4},{6,5},{7,6},{8,7},{9,8},{10,9... | collective-permute-start | bytes 147464 | tf_op jit(solution)/shard_map/ppermute | solution.py:530
  34.0 14.4 %collective-permute-start.19 = (f32[6,16,256]{2,1,0:T(8,128)S(1)}, f32[6,16,256]{2,1,0:T(8,128)S(1)}, u32[]{:S(2)}, u32[]{:S(2)}) collective-permute-start(f32[6,16,256]{2,1,0:T(8,128)S(1)} %get-tuple-element.1067), channel_id=1, source_target_pairs={{64,147},{128,76},{65,148},{129,77},{66,149},{130,78},{67,150},{13... | collective-permute-start | bytes 294920 | tf_op jit(solution)/shard_map/cond/branch_19_fun/ppermute | solution.py:560

commit v2 on v1

--- a/solution.py
+++ b/solution.py
@@ -58,6 +58,15 @@
     )
 
 
+def ghost_state_of(prim):
+    rho, u, press, nut = prim[0], prim[1:4], prim[4], prim[5]
+    kinetic = 0.5 * rho * (u[0] * u[0] + u[1] * u[1] + u[2] * u[2])
+    return dict(
+        rho=rho, m=[rho * v for v in u], u=u, p=press, e=press / (GAMMA - 1.0) + kinetic, n=rho * nut,
+        c=jnp.sqrt(GAMMA * press / rho),
+    )
+
+
 def cons_of(s):
     return [s["rho"], s["m"][0], s["m"][1], s["m"][2], s["e"], s["n"]]
 
@@ -73,6 +82,16 @@
     wave = jnp.maximum(jnp.abs(left["u"][k]) + left["c"], jnp.abs(right["u"][k]) + right["c"])
     return [
         (fl + fr) - wave * (ur - ul)
+        for fl, fr, ul, ur in zip(
+            flux_of(left, k), flux_of(right, k), cons_of(left), cons_of(right)
+        )
+    ]
+
+
+def ghost_face_of(left, right, k):
+    wave = jnp.maximum(jnp.abs(left["u"][k]) + left["c"], jnp.abs(right["u"][k]) + right["c"])
+    return [
+        0.5 * (fl + fr) - 0.5 * wave * (ur - ul)
         for fl, fr, ul, ur in zip(
             flux_of(left, k), flux_of(right, k), cons_of(left), cons_of(right)
         )
@@ -140,7 +159,8 @@
     for k in range(parts):
         for c in part_of(k):
             c.wait()
-        best = lax.fori_loop(k * CHUNK, (k + 1) * CHUNK, step, best)
+        for j in range(CHUNK):
+            best = step(k * CHUNK + j, best)
     largest = jnp.max(best, axis=0, keepdims=True)
     largest = jnp.max(largest, axis=1, keepdims=True)
     for v in range(6):
@@ -188,7 +208,7 @@
 
 
 def closure(rho, nut, dist, grad2):
-    square = jnp.maximum(0.25 * grad2, GRAD_FLOOR * GRAD_FLOOR)
+    square = jnp.maximum(grad2, GRAD_FLOOR * GRAD_FLOOR)
     inverse = lax.rsqrt(square)
     strain = square * inverse
     eight = (8.0 / (KAPPA * KAPPA)) * (nut + NU_LAM) * inverse / (dist * dist)
@@ -354,7 +374,7 @@
         for i in range(3):
             d = shifted["u%d" % i] - down_t(here["u"][i], pltpu.roll(azi_u[i], to_start, 1))
             grad2 = grad2 + d * d
-        shielding, source = closure(here["rho"], prim[5, a], wall[a], grad2)
+        shielding, source = closure(here["rho"], prim[5, a], wall[a], 0.25 * grad2)
         cons = cons_of(here)
         for i in range(5):
             flow[i, a] = cons[i] - half * total[i]
@@ -404,10 +424,10 @@
     step_size = edge[11]
     mine = [sent[v, :, :width] for v in range(6)]
     beyond = [jnp.where(coupled, ghost[v], mine[v]) for v in range(6)]
-    here, out_state = state_of(mine), state_of(beyond)
-    grad2 = edge[6]
+    here, out_state = state_of(mine), ghost_state_of(beyond)
+    grad2 = 0.25 * edge[6]
     for i in range(3):
-        d = edge[8 + i] - beyond[1 + i]
+        d = 0.5 * (edge[8 + i] - beyond[1 + i])
         grad2 = grad2 + d * d
 
     def pick(p, q):
@@ -420,8 +440,8 @@
 
     shielding, source = closure(here["rho"], mine[5], edge[7], grad2)
     edge_shield[...] = shielding
-    sign = jnp.where(even, -0.5, 0.5)
-    for i, f in enumerate(face_of(pick(out_state, here), pick(here, out_state), 0)):
+    sign = jnp.where(even, -1.0, 1.0)
+    for i, f in enumerate(ghost_face_of(pick(out_state, here), pick(here, out_state), 0)):
         value = edge[i] - step_size * (sign * f)
         edge_flow[i] = value + step_size * source if i == 5 else value
     copies = [

time: 49.1 us -> 48 us (0.978); the launches traced: 49.4 us -> 47.5 us
  starting transfers between devices: 34.2 us -> 33 us
  Pallas kernels: 10.3 us -> 9.49 us
    ppermute x1, starting transfers between devices: 8.62 us -> 7.44 us  [branch(): ghost = lax.ppermute(block, AXES, route)]
    pallas_call x1, Pallas kernels: 3.33 us -> 2.54 us  [derive_call(): pl.pallas_call(derive_kernel, out_shape=(plane, shaped(6, radial, width +...]
  transfers between devices with their start and end apart: 6 -> 6, of which waited for: 2 -> 2; matrix products, arithmetic and copies ran while one was open for 0% -> 0% of each run, Pallas kernels for 12% -> 13%
where the time goes in v2:
time: 48 us; the launch traced here: 47.5 us
  starting transfers between devices  33 us (69%)
  Pallas kernels  9.49 us (20%)
  waiting for transfers between devices  3.38 us (7%)
  between operations  1.52 us (3%)
    all_to_all x1, starting transfers between devices, body(): tops = lax.all_to_all(top, AXES, 0, 0)  14.8 us
    ppermute x1, starting transfers between devices, branch(): ghost = lax.ppermute(block, AXES, route)  7.44 us
    ppermute x1, starting transfers between devices, body(): col_next = lax.ppermute(cols, AXES, down)  6.24 us
    pallas_call x1, Pallas kernels, faces_call(): pl.pallas_call(face_kernel, out_shape=(apart(*whole), apart(count, radial...  5.77 us
    pallas_call x1, Pallas kernels, derive_call(): pl.pallas_call(derive_kernel, out_shape=(plane, shaped(6, radial, width +...  2.54 us
    all_to_all x1, waiting for transfers between devices, body(): tops = lax.all_to_all(top, AXES, 0, 0)  2.46 us
    ppermute x1, starting transfers between devices, body(): came = lax.ppermute(up_send, AXES, up)  2.2 us
    ppermute x1, starting transfers between devices, body(): swapped = lax.ppermute(moved, AXES, across)  1.47 us
  transfers between devices with their start and end apart: 6, of which 2 were waited for; matrix products, arithmetic and copies ran while one was open for 0% of the time, Pallas kernels for 13%

profile of v2, /device:TPU:1, one launch (start us, length us, event | category | flops | bytes accessed | tf_op | source)
XLA Modules:
  0.0 47.5 jit_solution(7140610964020214385)
XLA Ops:
  0.6 0.0 copy-start.1
  0.6 0.0 copy-start
  0.7 2.5 %derive.1 = (f32[6,16,256]{2,1,0:T(8,128)S(1)}, f32[6,16,384]{2,1,0:T(8,128)S(1)}, f32[6,16,256]{2,1,0:T(8,128)S(1)}, f32[6,16,256]{2,1,0:T(8,128)S(1)}, f32[6,1...) custom-call(f32[16,16,256]{2,1,0:T(8,128)} %rho_in.1, f32[3,16,16,256]{3,2,1,0:T(8,128)} %vel_in.1, ...), custom_call_target="tpu_custom_call" | custom-call | tf_op jit(solution)/shard_map/derive/pallas_call | solution.py:460
  3.2 2.2 %collective-permute-start.33 = (f32[6,16,384]{2,1,0:T(8,128)S(1)}, f32[6,16,384]{2,1,0:T(8,128)S(1)}, u32[]{:S(2)}, u32[]{:S(2)}) collective-permute-start(f32[6,16,384]{2,1,0:T(8,128)S(1)} %get-tuple-element.1259.sent), channel_id=1, source_target_pairs={{0,1},{1,2},{2,3},{3,4},{4,5},{5,6},{6,7},{7,8},{8,9},{9,10},{10,1... | collective-permute-start | bytes 442376 | tf_op jit(solution)/shard_map/ppermute | solution.py:549
  5.4 14.8 %all-to-all-start = ((f32[256,1,128]{2,1,0:T(1,128)}), f32[256,1,128]{2,1,0:T(1,128)S(1)}, u32[]{:S(2)}, u32[]{:S(2)}) async-start(f32[256,1,128]{2,1,0:T(1,128)} %get-tuple-element.1263), calls=%async_computation | async-start | bytes 262144 | tf_op jit(solution)/shard_map/all_to_all | solution.py:548
  20.9 0.0 collective-permute-done.33.came
  20.9 0.1 shift.2.own
  21.0 1.5 %collective-permute-start.34 = (f32[6,32,256]{2,1,0:T(8,128)S(1)}, f32[6,32,256]{2,1,0:T(8,128)S(1)}, u32[]{:S(2)}, u32[]{:S(2)}) collective-permute-start(f32[6,32,256]{2,1,0:T(8,128)S(1)} %shift.2.own), channel_id=1, source_target_pairs={{0,32},{1,33},{2,34},{3,35},{4,36},{5,37},{6,38},{7,39},{8,40},{9,... | collective-permute-start | bytes 589832 | tf_op jit(solution)/shard_map/ppermute | solution.py:561
  22.5 0.9 %collective-permute-start.32 = (f32[6,16,256]{2,1,0:T(8,128)S(1)}, f32[6,16,256]{2,1,0:T(8,128)S(1)}, u32[]{:S(2)}, u32[]{:S(2)}) collective-permute-start(f32[6,16,256]{2,1,0:T(8,128)S(1)} %get-tuple-element.1258), channel_id=1, source_target_pairs={{0,64},{1,65},{2,66},{3,67},{4,68},{5,69},{6,70},{7,71},{8,72},{9,... | collective-permute-start | bytes 294920 | tf_op jit(solution)/shard_map/ppermute | solution.py:551
  23.4 6.2 %collective-permute-start.35 = (f32[6,16,128]{2,1,0:T(8,128)S(1)}, f32[6,16,128]{2,1,0:T(8,128)S(1)}, u32[]{:S(2)}, u32[]{:S(2)}) collective-permute-start(f32[6,16,128]{2,1,0:T(8,128)S(1)} %get-tuple-element.1262), channel_id=1, source_target_pairs={{0,31},{1,0},{2,1},{3,2},{4,3},{5,4},{6,5},{7,6},{8,7},{9,8},{10,9... | collective-permute-start | bytes 147464 | tf_op jit(solution)/shard_map/ppermute | solution.py:550
  29.6 0.0 collective-permute-done.34.other
  29.6 0.0 copy-done.1
  29.6 0.0 copy-done
  29.6 0.3 weigh.1
  29.9 0.9 %collective-permute-done.35 = f32[6,16,128]{2,1,0:T(8,128)S(1)} collective-permute-done((f32[6,16,128]{2,1,0:T(8,128)S(1)}, f32[6,16,128]{2,1,0:T(8,128)S(1)}, u32[]{:S(2)}, u32[]{:S(2)}) %collective-permute-start.35) | collective-permute-done | bytes 49184 | tf_op jit(solution)/shard_map/ppermute | solution.py:550
  30.8 0.0 collective-permute-done.32
  30.8 2.5 %all-to-all-done = f32[256,1,128]{2,1,0:T(1,128)S(1)} async-done(((f32[256,1,128]{2,1,0:T(1,128)}), f32[256,1,128]{2,1,0:T(1,128)S(1)}, u32[]{:S(2)}, u32[]{:S(2)}) %all-to-all-start) | async-done | bytes 131104 | tf_op jit(solution)/shard_map/all_to_all | solution.py:548
  33.2 14.0 %conditional.1 = ((f32[6,16,16,256]{3,2,1,0:T(8,128)}, f32[16,16,256]{2,1,0:T(8,128)})) conditional(s32[]{:T(128)} %clamp.3, (f32[6,16,16,256]{3,2,1,0:T(8,128)S(1)}, f32[16,16,256]{2,1,0:T(8,128)}, f32[6,16,256]{2,1,0:T(8,128)S(1)}, f32[6,32,256]{2,1,0:T(8,128)S(1)}, f32[6,16,256]{2,1,0:T(8,128)S(1)}, ...), branch_computations={%region_0.1_spmd, %region_1.2_spmd, %region_2.3_spmd, %region_3.4_... | conditional | flops 25000000 | bytes 6393264 | solution.py:586
  33.2 7.4 %collective-permute-start.27 = (f32[6,16,256]{2,1,0:T(8,128)S(1)}, f32[6,16,256]{2,1,0:T(8,128)S(1)}, u32[]{:S(2)}, u32[]{:S(2)}) collective-permute-start(f32[6,16,256]{2,1,0:T(8,128)S(1)} %get-tuple-element.1187), channel_id=1, source_target_pairs={{64,155},{128,68},{65,156},{129,69},{66,157},{130,70},{67,158},{13... | collective-permute-start | bytes 294920 | tf_op jit(solution)/shard_map/cond/branch_27_fun/ppermute | solution.py:580
  40.7 5.8 %faces.59 = (f32[6,16,16,256]{3,2,1,0:T(8,128)}, f32[16,16,256]{2,1,0:T(8,128)}, f32[12,16,256]{2,1,0:T(8,128)S(1)}) custom-call(f32[6,16,16,256]{3,2,1,0:T(8,128)S(1)} %get-tuple-element.1173.prim, f32[16,16,256]{2,1,0:T(8,128)} %get-tuple-element.1174.wall_in, f32[6,16,256]{2,1,0:T(8,128)S(1)} %get-tuple-element.1175.core, ...), custom_call_target="tpu_custom_call" | custom-call | flops 25000000 | bytes 6000000 | tf_op jit(solution)/shard_map/cond/branch_27_fun/faces/pallas_call | solution.py:478
  46.5 0.0 collective-permute-done.27.ghost
  46.5 0.8 %edge.59 = (f32[6,16,16,256]{3,2,1,0:T(8,128)}, f32[16,16,256]{2,1,0:T(8,128)}) custom-call(f32[6,16,16,256]{3,2,1,0:T(8,128)} %get-tuple-element.1183.flow_in, f32[16,16,256]{2,1,0:T(8,128)} %get-tuple-element.1184.shield_in, f32[12,16,256]{2,1,0:T(8,128)S(1)} %get-tuple-element.1185.edge, ...), custom_call_target="tpu_custom_call", output_to_operand_aliasing={{0}: (0, {}), {1}: (1, {})} | custom-call | tf_op jit(solution)/shard_map/cond/branch_27_fun/edge/pallas_call | solution.py:508
Async XLA Ops:
  0.6 29.0 %copy-start.1 = (f32[16,32]{1,0:T(8,128)S(1)}, f32[16,32]{1,0:T(8,128)}, u32[]{:S(2)}) copy-start(f32[16,32]{1,0:T(8,128)} %back.1) | copy-start | bytes 6148
  0.6 29.0 %copy-start = (f32[16,32]{1,0:T(8,128)S(1)}, f32[16,32]{1,0:T(8,128)}, u32[]{:S(2)}) copy-start(f32[16,32]{1,0:T(8,128)} %fwd.1) | copy-start | bytes 6148
  3.2 17.7 %collective-permute-start.33 = (f32[6,16,384]{2,1,0:T(8,128)S(1)}, f32[6,16,384]{2,1,0:T(8,128)S(1)}, u32[]{:S(2)}, u32[]{:S(2)}) collective-permute-start(f32[6,16,384]{2,1,0:T(8,128)S(1)} %get-tuple-element.1259.sent), channel_id=1, source_target_pairs={{0,1},{1,2},{2,3},{3,4},{4,5},{5,6},{6,7},{7,8},{8,9},{9,10},{10,1... | collective-permute-start | bytes 442376 | tf_op jit(solution)/shard_map/ppermute | solution.py:549
  5.4 27.8 %all-to-all-start = ((f32[256,1,128]{2,1,0:T(1,128)}), f32[256,1,128]{2,1,0:T(1,128)S(1)}, u32[]{:S(2)}, u32[]{:S(2)}) async-start(f32[256,1,128]{2,1,0:T(1,128)} %get-tuple-element.1263), calls=%async_computation | async-start | bytes 262144 | tf_op jit(solution)/shard_map/all_to_all | solution.py:548
  21.0 8.6 %collective-permute-start.34 = (f32[6,32,256]{2,1,0:T(8,128)S(1)}, f32[6,32,256]{2,1,0:T(8,128)S(1)}, u32[]{:S(2)}, u32[]{:S(2)}) collective-permute-start(f32[6,32,256]{2,1,0:T(8,128)S(1)} %shift.2.own), channel_id=1, source_target_pairs={{0,32},{1,33},{2,34},{3,35},{4,36},{5,37},{6,38},{7,39},{8,40},{9,... | collective-permute-start | bytes 589832 | tf_op jit(solution)/shard_map/ppermute | solution.py:561
  22.5 8.3 %collective-permute-start.32 = (f32[6,16,256]{2,1,0:T(8,128)S(1)}, f32[6,16,256]{2,1,0:T(8,128)S(1)}, u32[]{:S(2)}, u32[]{:S(2)}) collective-permute-start(f32[6,16,256]{2,1,0:T(8,128)S(1)} %get-tuple-element.1258), channel_id=1, source_target_pairs={{0,64},{1,65},{2,66},{3,67},{4,68},{5,69},{6,70},{7,71},{8,72},{9,... | collective-permute-start | bytes 294920 | tf_op jit(solution)/shard_map/ppermute | solution.py:551
  23.4 7.4 %collective-permute-start.35 = (f32[6,16,128]{2,1,0:T(8,128)S(1)}, f32[6,16,128]{2,1,0:T(8,128)S(1)}, u32[]{:S(2)}, u32[]{:S(2)}) collective-permute-start(f32[6,16,128]{2,1,0:T(8,128)S(1)} %get-tuple-element.1262), channel_id=1, source_target_pairs={{0,31},{1,0},{2,1},{3,2},{4,3},{5,4},{6,5},{7,6},{8,7},{9,8},{10,9... | collective-permute-start | bytes 147464 | tf_op jit(solution)/shard_map/ppermute | solution.py:550
  33.2 13.2 %collective-permute-start.27 = (f32[6,16,256]{2,1,0:T(8,128)S(1)}, f32[6,16,256]{2,1,0:T(8,128)S(1)}, u32[]{:S(2)}, u32[]{:S(2)}) collective-permute-start(f32[6,16,256]{2,1,0:T(8,128)S(1)} %get-tuple-element.1187), channel_id=1, source_target_pairs={{64,155},{128,68},{65,156},{129,69},{66,157},{130,70},{67,158},{13... | collective-permute-start | bytes 294920 | tf_op jit(solution)/shard_map/cond/branch_27_fun/ppermute | solution.py:580
